TPU v7x, 128 devices: a whole 4x4x4 slice. The times are simulated.
128 devices in a mesh: shard: 4 (over y_lo, core), context: 8 (over y_hi, z), tensor: 4 (over x).
Axes of the slice: x: 4, y: 4 (y_hi: 2, y_lo: 2; y = y_hi * 2 + y_lo), z: 4, core: 2. Of those that a mesh axis runs over, the one named last changes fastest.
Arguments:
- inputs: bfloat16 [16, 1024, 2048], P('shard', 'context'), may hold values from -6 to 6
- cotangent: bfloat16 [16, 1024, 2048], P('shard', 'context'), may hold values from -6 to 6
- q_weight: bfloat16 [2048, 2048], P('shard', 'tensor'), may hold values from -0.125 to 0.125
- k_weight: bfloat16 [2048, 2048], P('shard', 'tensor'), may hold values from -0.125 to 0.125
- v_weight: bfloat16 [2048, 2048], P('shard', 'tensor'), may hold values from -0.125 to 0.125
- o_weight: bfloat16 [2048, 2048], P('tensor', 'shard'), may hold values from -2 to 2
- gate_weight: bfloat16 [2048, 8192], P('shard', 'tensor'), may hold values from -0.125 to 0.125
- up_weight: bfloat16 [2048, 8192], P('shard', 'tensor'), may hold values from -0.125 to 0.125
- down_weight: bfloat16 [8192, 2048], P('tensor', 'shard'), may hold values from -0.125 to 0.125
- attn_gain: bfloat16 [2048], P('shard'), may hold values from 0.099609375 to 1.8984375
- ffn_gain: bfloat16 [2048], P('shard'), may hold values from 0.099609375 to 1.8984375
- piece_starts: int32 [16, 2], P('shard'), may hold values from 0 to 768, as said below
- piece_ids: int32 [16, 2], P('shard'), may hold values from 0 to 1
- valid_mask: int32 [16, 1024], P('shard'), may hold values from 0 to 1, as said below
Outputs:
- output: bfloat16 [16, 1024, 2048], P('shard', 'context')
- input_grad: bfloat16 [16, 1024, 2048], P('shard', 'context')
- q_grad: float32 [2048, 2048], P('shard', 'tensor')
- k_grad: float32 [2048, 2048], P('shard', 'tensor')
- v_grad: float32 [2048, 2048], P('shard', 'tensor')
- o_grad: float32 [2048, 2048], P('tensor', 'shard')
- gate_grad: float32 [2048, 8192], P('shard', 'tensor')
- up_grad: float32 [2048, 8192], P('shard', 'tensor')
- down_grad: float32 [8192, 2048], P('tensor', 'shard')
- attn_gain_grad: float32 [2048], P(('shard', 'tensor'))
- ffn_gain_grad: float32 [2048], P(('shard', 'tensor'))
- branch_rms: float32 [3], replicated
Inputs may be any that keep to these rules, and one draw needn't show every extreme that they name: `piece_starts`: the 2 pieces of a sequence do not intersection: piece p starts between p * 512 and (p + 1) * 512 - 256. `piece_ids`: pieces of one sequence with equal ids show one picture. `valid_mask`: the real tokens of a sequence are a prefix of 256 to 1024 tokens; both lengths occur in every draw.
All inputs are finite; a program needn't handle non-finite values.
Results may differ from a plain program's by a relative error of at most 0.03.
Values may be sent and summed in bfloat16 or wider, within the bound.
A program may use at most 256 MiB of HBM per device.

v0:
```python
import jax
import jax.numpy as jnp
from jax import lax
from jax.sharding import PartitionSpec as P

HEAD_DIM = 64
PIECE = 256


NORM_EPS = 1e-05
ROPE_BASE = 130000.0
MASK_FILL = -1e30


def gather_turned(arrays, axis, dims):
    turned = [jnp.moveaxis(a, dim, 0) for a, dim in zip(arrays, dims)]
    widths = [t[0].size for t in turned]
    both = jnp.concatenate([t.reshape(-1, w) for t, w in zip(turned, widths)], axis=1)
    filled = lax.all_gather(both, axis, axis=0, tiled=True)
    parts = jnp.split(filled, [sum(widths[:k]) for k in range(1, len(widths))], axis=1)
    return tuple(
        (
            jnp.moveaxis(b.reshape(-1, *t.shape[1:]), 0, dim)
            for b, t, dim in zip(parts, turned, dims)
        )
    )


def sent_together(arrays, axis, dim, along):
    both = jnp.concatenate(arrays, axis=along)
    filled, at, gathered = (lax.all_gather(both, axis, axis=dim, tiled=True), 0, [])
    for a in arrays:
        gathered.append(lax.slice_in_dim(filled, at, at + a.shape[along], axis=along))
        at += a.shape[along]
    return tuple(gathered)


def from_everyone(x, axis):
    copies = jnp.broadcast_to(x, (lax.axis_size(axis), *x.shape))
    return lax.all_to_all(copies, axis, split_axis=0, concat_axis=0, tiled=True)


def of_everyone(x, axis):
    everything = from_everyone(x, axis)
    return jnp.sum(everything, axis=0)


def in_one_piece(arrays, axis, dim, along):
    widths = [a.shape[along] for a in arrays]
    both = jnp.concatenate(arrays, axis=along)
    filled = lax.psum_scatter(both, axis, scatter_dimension=dim, tiled=True)
    return tuple(jnp.split(filled, [sum(widths[:k]) for k in range(1, len(widths))], axis=along))


def packed_total(arrays, axis):
    vector, at, gathered = (jnp.concatenate([a.reshape(-1) for a in arrays]), 0, [])
    subtotal = lax.psum(vector, axis)
    for a in arrays:
        gathered.append(subtotal[at : at + a.size].reshape(a.shape))
        at += a.size
    return tuple(gathered)


def rope_tables(positions, head_size):
    half_dim = head_size // 2
    inv_freq = ROPE_BASE ** (-jnp.arange(half_dim, dtype=jnp.float32) * 2.0 / head_size)
    angles = positions.astype(jnp.float32)[:, None] * inv_freq[None, :]
    angles = jnp.concatenate([angles, angles], axis=1)
    return (jnp.cos(angles), jnp.sin(angles))


def rotate(values, cosine, sine_tab):
    row_count, col_count = values.shape
    head_size = cosine.shape[1]
    half_dim = head_size // 2
    split_heads = values.reshape(row_count, col_count // head_size, head_size)
    turned = jnp.concatenate([-split_heads[:, :, half_dim:], split_heads[:, :, :half_dim]], axis=2)
    return (split_heads * cosine[:, None, :] + turned * sine_tab[:, None, :]).reshape(
        row_count, col_count
    )


def unrotate(grads_in, cosine, sine_tab):
    row_count, col_count = grads_in.shape
    head_size = cosine.shape[1]
    half_dim = head_size // 2
    split_heads = grads_in.reshape(row_count, col_count // head_size, head_size)
    scaled = split_heads * sine_tab[:, None, :]
    turned = jnp.concatenate([scaled[:, :, half_dim:], -scaled[:, :, :half_dim]], axis=2)
    return (split_heads * cosine[:, None, :] + turned).reshape(row_count, col_count)


def piece_index(starts, piece_tags, positions):
    inside = (positions[None, :, None] >= starts[:, None, :]) & (
        positions[None, :, None] < starts[:, None, :] + PIECE
    )
    tagged = jnp.where(inside, piece_tags[:, None, :] + 1, 0)
    return jnp.sum(tagged, axis=2) - 1


def rms_scale(values):
    return lax.rsqrt(jnp.mean(values * values, axis=1, keepdims=True) + NORM_EPS)


def norm_back(grad_out, normed, gain, inv_rms):
    scaled = grad_out * gain
    return inv_rms * (scaled - normed * jnp.mean(scaled * normed, axis=1, keepdims=True))


def matmul_low(left, right):
    return jnp.dot(left, right, preferred_element_type=jnp.float32)


def per_device(
    inputs,
    cotangent,
    q_weight,
    k_weight,
    v_weight,
    o_weight,
    gate_weight,
    up_weight,
    down_weight,
    attn_gain,
    ffn_gain,
    piece_starts,
    piece_ids,
    valid_mask,
):
    seq_count, block_len, model_width = inputs.shape
    seq_length = valid_mask.shape[1]
    token_rows = seq_count * block_len
    score_scale = HEAD_DIM ** (-0.5)
    block_start = lax.axis_index("context") * block_len
    own_pos = block_start + jnp.arange(block_len, dtype=jnp.int32)
    all_pos = jnp.arange(seq_length, dtype=jnp.int32)
    cosine, sine_tab = rope_tables(jnp.tile(own_pos, seq_count), HEAD_DIM)
    query_piece = piece_index(piece_starts, piece_ids, own_pos)
    key_piece = piece_index(piece_starts, piece_ids, all_pos)
    causal = all_pos[None, None, :] <= own_pos[None, :, None]
    same_pic = (query_piece[:, :, None] >= 0) & (query_piece[:, :, None] == key_piece[:, None, :])
    visible = (valid_mask[:, None, :] > 0) | (all_pos[None, None, :] == own_pos[None, :, None])
    allowed = (causal | same_pic) & visible
    valid_own = lax.dynamic_slice_in_dim(valid_mask, block_start, block_len, 1)
    q_full, k_full, v_full, o_full, gate_full, up_full, down_full, gain_attn, gain_ffn = (
        gather_turned(
            (
                q_weight,
                k_weight,
                v_weight,
                o_weight,
                gate_weight,
                up_weight,
                down_weight,
                attn_gain,
                ffn_gain,
            ),
            "shard",
            (0, 0, 0, 1, 0, 0, 1, 0, 0),
        )
    )
    gain_attn_f = gain_attn.astype(jnp.float32)
    gain_ffn_f = gain_ffn.astype(jnp.float32)
    x_rows = inputs.reshape(token_rows, model_width).astype(jnp.float32)
    rsqrt_attn = rms_scale(x_rows)
    normed_attn = x_rows * rsqrt_attn
    attn_in = (normed_attn * gain_attn_f).astype(jnp.bfloat16)
    query_rot = rotate(matmul_low(attn_in, q_full), cosine, sine_tab).astype(jnp.bfloat16)
    key_rot = rotate(matmul_low(attn_in, k_full), cosine, sine_tab).astype(jnp.bfloat16)
    value_rows = matmul_low(attn_in, v_full).astype(jnp.bfloat16)
    head_cols = query_rot.shape[1]
    local_heads = head_cols // HEAD_DIM
    key_all, value_all = sent_together(
        (
            key_rot.reshape(seq_count, block_len, head_cols),
            value_rows.reshape(seq_count, block_len, head_cols),
        ),
        "context",
        1,
        0,
    )

    def to_heads(values, span):
        return values.reshape(seq_count, span, local_heads, HEAD_DIM).transpose(2, 0, 1, 3)

    def from_heads(values, span):
        return values.transpose(1, 2, 0, 3).reshape(seq_count, span, head_cols)

    query_split = to_heads(query_rot, block_len)
    key_split = to_heads(key_all, seq_length)
    value_split = to_heads(value_all, seq_length)

    def head_scores(query_h, key_h):
        score = score_scale * jnp.einsum(
            "sqd,skd->sqk", query_h, key_h, preferred_element_type=jnp.float32
        )
        return jnp.where(allowed, score, MASK_FILL)

    def attend(head_item):
        query_h, key_h, value_h = head_item
        score = head_scores(query_h, key_h)
        row_top = jnp.max(score, axis=2, keepdims=True)
        row_total = row_top + jnp.log(jnp.sum(jnp.exp(score - row_top), axis=2, keepdims=True))
        attn_prob = jnp.exp(score - row_total).astype(jnp.bfloat16)
        head_mix = jnp.einsum(
            "sqk,skd->sqd", attn_prob, value_h, preferred_element_type=jnp.float32
        )
        return (head_mix, row_total[:, :, 0])

    head_mix, row_totals = lax.map(attend, (query_split, key_split, value_split))
    attended = from_heads(head_mix, block_len).reshape(token_rows, head_cols).astype(jnp.bfloat16)
    attn_out = lax.psum(matmul_low(attended, o_full), "tensor")
    resid = x_rows + attn_out
    rsqrt_ffn = rms_scale(resid)
    normed_ffn = resid * rsqrt_ffn
    ffn_in = (normed_ffn * gain_ffn_f).astype(jnp.bfloat16)
    gate_val = matmul_low(ffn_in, gate_full)
    up_val = matmul_low(ffn_in, up_full)
    hidden = (jax.nn.silu(gate_val) * up_val).astype(jnp.bfloat16)
    ffn_out = lax.psum(matmul_low(hidden, down_full).astype(jnp.bfloat16), "tensor").astype(
        jnp.float32
    )
    final_out = resid + ffn_out
    output = final_out.astype(jnp.bfloat16).reshape(seq_count, block_len, model_width)
    keep_rows = valid_own.reshape(token_rows, 1).astype(jnp.float32)
    stat_local = jnp.stack(
        [
            jnp.sum(keep_rows),
            jnp.sum(keep_rows * attn_out * attn_out),
            jnp.sum(keep_rows * ffn_out * ffn_out),
            jnp.sum(keep_rows * final_out * final_out),
        ]
    )
    stat_sums = of_everyone(stat_local, ("shard", "context"))
    branch_rms = jnp.sqrt(stat_sums[1:] / (jnp.maximum(stat_sums[0], 1.0) * model_width))
    q_back, k_back, v_back, o_back, gate_back, up_back, down_back = (
        q_full,
        k_full,
        v_full,
        o_full,
        gate_full,
        up_full,
        down_full,
    )
    grad_rows = cotangent.reshape(token_rows, model_width)
    down_grad = jnp.einsum("nf,nd->fd", hidden, grad_rows, preferred_element_type=jnp.float32)
    grad_hidden = jnp.einsum("nd,fd->nf", grad_rows, down_back, preferred_element_type=jnp.float32)
    gate_sig = jax.nn.sigmoid(gate_val)
    grad_gate = (grad_hidden * up_val * gate_sig * (1.0 + gate_val * (1.0 - gate_sig))).astype(
        jnp.bfloat16
    )
    grad_up = (grad_hidden * jax.nn.silu(gate_val)).astype(jnp.bfloat16)
    gate_grad = jnp.einsum("nd,nf->df", ffn_in, grad_gate, preferred_element_type=jnp.float32)
    up_grad = jnp.einsum("nd,nf->df", ffn_in, grad_up, preferred_element_type=jnp.float32)
    ffn_in_part = jnp.einsum(
        "nf,df->nd", grad_gate, gate_back, preferred_element_type=jnp.float32
    ) + jnp.einsum("nf,df->nd", grad_up, up_back, preferred_element_type=jnp.float32)
    grad_ffn_in = lax.psum(ffn_in_part, "tensor")
    ffn_gain_grad = jnp.sum(grad_ffn_in * normed_ffn, axis=0)
    grad_resid = grad_rows.astype(jnp.float32) + norm_back(
        grad_ffn_in, normed_ffn, gain_ffn_f, rsqrt_ffn
    )
    grad_attn = grad_resid.astype(jnp.bfloat16)
    o_grad = jnp.einsum("nc,nd->cd", attended, grad_attn, preferred_element_type=jnp.float32)
    grad_attended = jnp.einsum(
        "nd,cd->nc", grad_attn, o_back, preferred_element_type=jnp.float32
    ).astype(jnp.bfloat16)
    grad_split = to_heads(grad_attended, block_len)

    def query_side(head_item):
        query_h, key_h, value_h, grad_h, total_h = head_item
        score = head_scores(query_h, key_h)
        attn_prob = jnp.exp(score - total_h[:, :, None])
        grad_prob = jnp.einsum("sqd,skd->sqk", grad_h, value_h, preferred_element_type=jnp.float32)
        inner = jnp.sum(attn_prob * grad_prob, axis=2, keepdims=True)
        grad_score = (attn_prob * (grad_prob - inner)).astype(jnp.bfloat16)
        grad_query_h = score_scale * jnp.einsum(
            "sqk,skd->sqd", grad_score, key_h, preferred_element_type=jnp.float32
        )
        return (grad_query_h, inner[:, :, 0])

    grad_query_heads, inner_rows = lax.map(
        query_side, (query_split, key_split, value_split, grad_split, row_totals)
    )
    query_every, grad_every = sent_together(
        (
            query_rot.reshape(seq_count, block_len, head_cols),
            grad_attended.reshape(seq_count, block_len, head_cols),
        ),
        "context",
        1,
        0,
    )
    total_every, inner_every = sent_together((row_totals, inner_rows), "context", 2, 0)
    causal_kv = own_pos[None, None, :] <= all_pos[None, :, None]
    same_pic_kv = (key_piece[:, :, None] >= 0) & (key_piece[:, :, None] == query_piece[:, None, :])
    visible_kv = (valid_own[:, None, :] > 0) | (own_pos[None, None, :] == all_pos[None, :, None])
    allowed_kv = (causal_kv | same_pic_kv) & visible_kv

    def key_side(head_item):
        query_h, key_h, value_h, grad_h, total_h, inner_h = head_item
        score = score_scale * jnp.einsum(
            "sqd,skd->sqk", query_h, key_h, preferred_element_type=jnp.float32
        )
        score = jnp.where(allowed_kv, score, MASK_FILL)
        attn_prob = jnp.exp(score - total_h[:, :, None])
        grad_prob = jnp.einsum("sqd,skd->sqk", grad_h, value_h, preferred_element_type=jnp.float32)
        grad_score = (attn_prob * (grad_prob - inner_h[:, :, None])).astype(jnp.bfloat16)
        grad_key_h = score_scale * jnp.einsum(
            "sqk,sqd->skd", grad_score, query_h, preferred_element_type=jnp.float32
        )
        grad_value_h = jnp.einsum(
            "sqk,sqd->skd",
            attn_prob.astype(jnp.bfloat16),
            grad_h,
            preferred_element_type=jnp.float32,
        )
        return (grad_key_h, grad_value_h)

    grad_key_heads, grad_value_heads = lax.map(
        key_side,
        (
            to_heads(query_every, seq_length),
            to_heads(key_rot, block_len),
            to_heads(value_rows, block_len),
            to_heads(grad_every, seq_length),
            total_every,
            inner_every,
        ),
    )
    key_grad_own = from_heads(grad_key_heads, block_len)
    value_grad_own = from_heads(grad_value_heads, block_len)
    grad_key = unrotate(key_grad_own.reshape(token_rows, head_cols), cosine, sine_tab).astype(
        jnp.bfloat16
    )
    grad_value = value_grad_own.reshape(token_rows, head_cols).astype(jnp.bfloat16)
    grad_query = unrotate(
        from_heads(grad_query_heads, block_len).reshape(token_rows, head_cols), cosine, sine_tab
    ).astype(jnp.bfloat16)
    q_grad = jnp.einsum("nd,nc->dc", attn_in, grad_query, preferred_element_type=jnp.float32)
    k_grad = jnp.einsum("nd,nc->dc", attn_in, grad_key, preferred_element_type=jnp.float32)
    v_grad = jnp.einsum("nd,nc->dc", attn_in, grad_value, preferred_element_type=jnp.float32)
    attn_in_part = jnp.einsum("nc,dc->nd", grad_query, q_back, preferred_element_type=jnp.float32)
    attn_in_part = attn_in_part + jnp.einsum(
        "nc,dc->nd", grad_key, k_back, preferred_element_type=jnp.float32
    )
    attn_in_part = attn_in_part + jnp.einsum(
        "nc,dc->nd", grad_value, v_back, preferred_element_type=jnp.float32
    )
    grad_attn_in = lax.psum(attn_in_part.astype(jnp.bfloat16), "tensor").astype(jnp.float32)
    attn_gain_grad = jnp.sum(grad_attn_in * normed_attn, axis=0)
    grad_input = grad_resid + norm_back(grad_attn_in, normed_attn, gain_attn_f, rsqrt_attn)
    input_grad = grad_input.astype(jnp.bfloat16).reshape(seq_count, block_len, model_width)
    grad_parts = (
        q_grad,
        k_grad,
        v_grad,
        o_grad,
        gate_grad,
        up_grad,
        down_grad,
        attn_gain_grad,
        ffn_gain_grad,
    )
    reduced = (
        *tuple(
            (
                part.astype(jnp.float32)
                for part in in_one_piece(
                    (
                        grad_parts[0].astype(jnp.bfloat16),
                        grad_parts[1].astype(jnp.bfloat16),
                        grad_parts[2].astype(jnp.bfloat16),
                    ),
                    "shard",
                    0,
                    1,
                )
            )
        ),
        lax.psum_scatter(
            grad_parts[3].astype(jnp.bfloat16), "shard", scatter_dimension=1, tiled=True
        ).astype(jnp.float32),
        *tuple(
            (
                part.astype(jnp.float32)
                for part in in_one_piece(
                    (grad_parts[4].astype(jnp.bfloat16), grad_parts[5].astype(jnp.bfloat16)),
                    "shard",
                    0,
                    1,
                )
            )
        ),
        lax.psum_scatter(
            grad_parts[6].astype(jnp.bfloat16), "shard", scatter_dimension=1, tiled=True
        ).astype(jnp.float32),
        lax.psum_scatter(
            grad_parts[7].astype(jnp.bfloat16), "shard", scatter_dimension=0, tiled=True
        ).astype(jnp.float32),
        lax.psum_scatter(
            grad_parts[8].astype(jnp.bfloat16), "shard", scatter_dimension=0, tiled=True
        ).astype(jnp.float32),
    )
    summed = tuple(
        (
            part.astype(jnp.float32)
            for part in packed_total(
                (
                    reduced[0].astype(jnp.bfloat16),
                    reduced[1].astype(jnp.bfloat16),
                    reduced[2].astype(jnp.bfloat16),
                    reduced[3].astype(jnp.bfloat16),
                    reduced[4].astype(jnp.bfloat16),
                    reduced[5].astype(jnp.bfloat16),
                    reduced[6].astype(jnp.bfloat16),
                    reduced[7].astype(jnp.bfloat16),
                    reduced[8].astype(jnp.bfloat16),
                ),
                "context",
            )
        )
    )
    gain_share = summed[7].shape[0] // lax.axis_size("tensor")
    gain_start = lax.axis_index("tensor") * gain_share
    attn_gain_out = lax.dynamic_slice_in_dim(summed[7], gain_start, gain_share, 0)
    ffn_gain_out = lax.dynamic_slice_in_dim(summed[8], gain_start, gain_share, 0)
    return (
        output,
        input_grad,
        summed[0],
        summed[1],
        summed[2],
        summed[3],
        summed[4],
        summed[5],
        summed[6],
        attn_gain_out,
        ffn_gain_out,
        branch_rms,
    )


def solution(mesh):
    return jax.shard_map(
        per_device,
        mesh=mesh,
        in_specs=(
            P("shard", "context", None),
            P("shard", "context", None),
            P("shard", "tensor"),
            P("shard", "tensor"),
            P("shard", "tensor"),
            P("tensor", "shard"),
            P("shard", "tensor"),
            P("shard", "tensor"),
            P("tensor", "shard"),
            P("shard"),
            P("shard"),
            P("shard", None),
            P("shard", None),
            P("shard", None),
        ),
        out_specs=(
            P("shard", "context", None),
            P("shard", "context", None),
            P("shard", "tensor"),
            P("shard", "tensor"),
            P("shard", "tensor"),
            P("tensor", "shard"),
            P("shard", "tensor"),
            P("shard", "tensor"),
            P("tensor", "shard"),
            P(("shard", "tensor")),
            P(("shard", "tensor")),
            P(),
        ),
        check_vma=False,
    )
```

profile of v0, /device:TPU:1, one launch (start us, length us, event | category | flops | bytes accessed | tf_op | source)
XLA Modules:
  0.0 1589.0 jit_solution(13492141286229071972)
XLA Ops:
  18.6 34.0 %concatenate.48 = bf16[512,8194]{0,1:T(8,128)(2,1)} concatenate(bf16[512,512]{0,1:T(8,128)(2,1)S(1)} %copy.157, bf16[512,512]{0,1:T(8,128)(2,1)S(1)} %copy.158, bf16[512,512]{0,1:T(8,128)(2,1)} %copy.159, bf16[512,512]{0,1:T(8,128)(2,1)} %bitcast.380, bf16[512,2048]{0,1:T(8,128)(2,1)S(1)} %copy.160, bf16[512,2048]{0,1:T(8,128)(2,1)} %copy.161, bf16[512,2048]{0,1:T(8,128)(2,1)} %bitcast.350, ...), dimensions={1} | concatenate | bytes 16781312 | tf_op jit(solution)/shard_map/concatenate | solution.py:18
  54.8 295.4 %all-gather.4.cloned.1.call-done = bf16[2048,8194]{0,1:T(8,128)(2,1)} async-done(((bf16[512,8194]{0,1:T(8,128)(2,1)}), bf16[2048,8194]{0,1:T(8,128)(2,1)}) %all-gather.4.cloned.1.call-update) | async-done | bytes 33562640 | tf_op jit(solution)/shard_map/all_gather | solution.py:19
  374.4 111.1 %all-gather.6.cloned.1.call-done = bf16[8,1024,512]{1,2,0:T(8,128)(2,1)} async-done(((bf16[8,128,512]{1,2,0:T(8,128)(2,1)}), bf16[8,1024,512]{1,2,0:T(8,128)(2,1)}) %all-gather.6.cloned.1.call-update) | async-done | bytes 8388624 | tf_op jit(solution)/shard_map/all_gather | solution.py:31
  494.3 34.9 %while.39 = (s32[]{:T(128)}, bf16[8,4,128,64]{2,3,1,0:T(8,128)(2,1)S(1)}, f32[8,4,128]{2,1,0:T(4,128)S(1)}, bf16[8,4,128,64]{2,3,1,0:T(8,128)(2,1)}, bf16[8,4,10...) while((s32[]{:T(128)}, ...), condition=%wide.region_6.7_spmd.clone, body=%wide.region_3.6_spmd.clone.sunk | while | flops 140508672 | bytes 7840393 | solution.py:210
  535.4 10.5 fusion.54
  545.9 80.5 %all-reduce.9.cloned.1.call-done = f32[512,2048]{1,0:T(8,128)} async-done(((f32[512,2048]{1,0:T(8,128)}), f32[512,2048]{1,0:T(8,128)}) %all-reduce.9.cloned.1.call-update) | async-done | bytes 4194320 | tf_op jit(solution)/shard_map/psum | solution.py:212
  631.7 7.8 fusion.64
  639.4 9.5 fusion.78
  650.3 9.1 fusion.90
  667.5 9.7 fusion.87
  678.4 39.7 %all-reduce.11.cloned.1.call-done = bf16[512,2048]{1,0:T(8,128)(2,1)} async-done(((bf16[512,2048]{1,0:T(8,128)(2,1)}), bf16[512,2048]{1,0:T(8,128)(2,1)}) %all-reduce.11.cloned.1.call-update) | async-done | bytes 2097168 | tf_op jit(solution)/shard_map/psum | solution.py:220
  718.1 94.8 %all-reduce.13.cloned.1.call-done = f32[512,2048]{1,0:T(8,128)} async-done(((f32[512,2048]{1,0:T(8,128)}), f32[512,2048]{1,0:T(8,128)}) %all-reduce.13.cloned.1.call-update) | async-done | bytes 4194320 | tf_op jit(solution)/shard_map/psum | solution.py:258
  812.9 8.9 fusion.73
  838.0 10.5 convolution_convert_fusion
  849.1 45.9 %while.40 = (s32[]{:T(128)}, f32[8,4,128,64]{2,3,1,0:T(8,128)S(1)}, f32[8,4,128]{2,1,0:T(4,128)S(1)}, bf16[8,4,128,64]{2,3,1,0:T(8,128)(2,1)}, bf16[8,4,1024,64]...) while((s32[]{:T(128)}, f32[8,4,128,64]{2,3,1,0:T(8,128)S(1)}, ...), condition=%wide.region_14.15_spmd.clone, body=%wide.region_12.14_spmd.clone.sunk | while | flops 208174592 | bytes 12753573 | solution.py:282
  896.7 29.8 %all_gather.15 = f32[16,4,1024]{2,1,0:T(4,128)S(1)} all-gather(f32[16,4,128]{2,1,0:T(4,128)S(1)} %pad_maximum_fusion.7), channel_id=1, replica_groups=mesh['shard'=4,'context'=8,'tensor'=4] {'context'}, dimensions={2}, use_global_device_ids=true | all-gather | bytes 294912 | tf_op jit(solution)/shard_map/all_gather | solution.py:31
  927.2 19.5 %all-gather.8.cloned.1.call-done = bf16[8,1024,512]{1,2,0:T(8,128)(2,1)} async-done(((bf16[8,128,512]{1,2,0:T(8,128)(2,1)}), bf16[8,1024,512]{1,2,0:T(8,128)(2,1)}) %all-gather.8.cloned.1.call-update) | async-done | bytes 8388624 | tf_op jit(solution)/shard_map/all_gather | solution.py:31
  953.9 82.5 %while.41 = (s32[]{:T(128)}, f32[8,4,128,64]{2,3,1,0:T(8,128)}, bf16[8,4,128,64]{2,3,1,0:T(8,128)(2,1)}, bf16[8,4,1024,64]{2,3,0,1:T(8,128)(2,1)}, bf16[8,4,128,...) while((s32[]{:T(128)}, f32[8,4,128,64]{2,3,1,0:T(8,128)}, ...), condition=%wide.region_16.17_spmd.clone, body=%wide.region_15.16_spmd.clone.sunk | while | flops 274759680 | bytes 9300133 | solution.py:320
  1058.5 11.4 pad_maximum_fusion.1
  1097.8 23.0 %all-reduce.15.cloned.1.call-done = bf16[512,2048]{1,0:T(8,128)(2,1)} async-done(((bf16[512,2048]{1,0:T(8,128)(2,1)}), bf16[512,2048]{1,0:T(8,128)(2,1)}) %all-reduce.15.cloned.1.call-update) | async-done | bytes 2097168 | tf_op jit(solution)/shard_map/psum | solution.py:350
  1129.6 56.1 %reduce-scatter.5.cloned.1.call-done = bf16[512,1536]{0,1:T(8,128)(2,1)} async-done(((bf16[2048,1536]{0,1:T(8,128)(2,1)}), bf16[512,1536]{0,1:T(8,128)(2,1)}) %reduce-scatter.5.cloned.1.call-update) | async-done | bytes 1572880 | tf_op jit(solution)/shard_map/reduce_scatter | solution.py:51
  1202.2 133.6 %reduce-scatter.9.cloned.1.call-done = bf16[512,4096]{0,1:T(8,128)(2,1)} async-done(((bf16[2048,4096]{0,1:T(8,128)(2,1)}), bf16[512,4096]{0,1:T(8,128)(2,1)}) %reduce-scatter.9.cloned.1.call-update) | async-done | bytes 4194320 | tf_op jit(solution)/shard_map/reduce_scatter | solution.py:51
  1386.2 162.9 %all-reduce.17.cloned.1.call-done = bf16[4195328]{0:T(1024)(128)(2,1)} async-done(((bf16[4195328]{0:T(1024)(128)(2,1)}), bf16[4195328]{0:T(1024)(128)(2,1)}) %all-reduce.17.cloned.1.call-update) | async-done | bytes 8390672 | tf_op jit(solution)/shard_map/psum | solution.py:57
  1557.5 7.8 slice_convert_fusion
  (377 shorter events, 406.6 us)
Async XLA Ops:
  7.2 343.0 %all-gather.4.cloned.1.call-start = ((), (), s32[]{:S(2)}) async-start(), calls=%async_computation.5 | async-start | bytes 41984000 | tf_op jit(solution)/shard_map/all_gather | solution.py:19
  52.7 432.8 %all-gather.6.cloned.1.call-start = ((), (), s32[]{:S(2)}) async-start(), calls=%async_computation.6 | async-start | bytes 9437184 | tf_op jit(solution)/shard_map/all_gather | solution.py:31
  54.3 312.3 %copy-start.17 = (f32[512,64]{0,1:T(8,128)}, f32[512,64]{0,1:T(8,128)S(1)}, u32[]{:S(2)}) copy-start(f32[512,64]{0,1:T(8,128)S(1)} %get-tuple-element.582) | copy-start | bytes 393220
  54.3 312.3 %copy-start.25 = (f32[512,64]{0,1:T(8,128)}, f32[512,64]{0,1:T(8,128)S(1)}, u32[]{:S(2)}) copy-start(f32[512,64]{0,1:T(8,128)S(1)} %get-tuple-element.583) | copy-start | bytes 393220
  54.8 303.9 %copy-start.31 = (f32[512]{0:T(512)}, f32[512]{0:T(512)S(1)}, u32[]{:S(2)}) copy-start(f32[512]{0:T(512)S(1)} %get-tuple-element.584) | copy-start | bytes 6148
  371.6 254.8 %all-reduce.9.cloned.1.call-start = ((), (), s32[]{:S(2)}) async-start(), calls=%async_computation.7 | async-start | bytes 8388608 | tf_op jit(solution)/shard_map/psum | solution.py:212
  372.0 117.5 %copy-start.9 = (bf16[8,4,128,64]{2,3,1,0:T(8,128)(2,1)}, bf16[8,4,128,64]{2,3,1,0:T(8,128)(2,1)S(1)}, u32[]{:S(2)}) copy-start(bf16[8,4,128,64]{2,3,1,0:T(8,128)(2,1)S(1)} %fusion.145) | copy-start | bytes 1572868
  535.3 182.8 %all-reduce.11.cloned.1.call-start = ((), (), s32[]{:S(2)}) async-start(), calls=%async_computation.8 | async-start | bytes 4194304 | tf_op jit(solution)/shard_map/psum | solution.py:220
  659.4 153.5 %all-reduce.13.cloned.1.call-start = ((), (), s32[]{:S(2)}) async-start(), calls=%async_computation.9 | async-start | bytes 8388608 | tf_op jit(solution)/shard_map/psum | solution.py:258
  677.2 269.6 %all-gather.8.cloned.1.call-start = ((), (), s32[]{:S(2)}) async-start(), calls=%async_computation.10 | async-start | bytes 9437184 | tf_op jit(solution)/shard_map/all_gather | solution.py:31
  678.4 143.4 %copy-start.24 = (bf16[4,128,2048]{2,1,0:T(8,128)(2,1)S(1)}, bf16[4,128,2048]{2,1,0:T(8,128)(2,1)}, u32[]{:S(2)}) copy-start(bf16[4,128,2048]{2,1,0:T(8,128)(2,1)} %param.21) | copy-start | bytes 6291460
  828.8 263.7 %reduce-scatter.7.cloned.1.call-start = ((), (), s32[]{:S(2)}) async-start(), calls=%async_computation.13 | async-start | bytes 2621440 | tf_op jit(solution)/shard_map/reduce_scatter | solution.py:381
  833.7 260.1 %reduce-scatter.11.cloned.1.call-start = ((), (), s32[]{:S(2)}) async-start(), calls=%async_computation.15 | async-start | bytes 10485760 | tf_op jit(solution)/shard_map/reduce_scatter | solution.py:395
  848.6 272.2 %all-reduce.15.cloned.1.call-start = ((), (), s32[]{:S(2)}) async-start(), calls=%async_computation.11 | async-start | bytes 4194304 | tf_op jit(solution)/shard_map/psum | solution.py:350
  895.0 57.8 %copy-start.34 = (s32[4,1024]{1,0:T(4,128)}, s32[4,1024]{1,0:T(4,128)S(1)}, u32[]{:S(2)}) copy-start(s32[4,1024]{1,0:T(4,128)S(1)} %get-tuple-element.1047) | copy-start | bytes 49156
  927.2 26.7 %copy-start.42 = (pred[4,128]{1,0:T(4,128)(4,1)S(1)}, pred[4,128]{1,0:T(4,128)(4,1)}, u32[]{:S(2)}) copy-start(pred[4,128]{1,0:T(4,128)(4,1)} %dynamic-slice_compare_fusion) | copy-start | bytes 1540
  953.9 85.9 %copy-start.26 = (f32[512,64]{0,1:T(8,128)S(1)}, f32[512,64]{0,1:T(8,128)}, u32[]{:S(2)}) copy-start(f32[512,64]{0,1:T(8,128)} %copy-done.25) | copy-start | bytes 393220
  1054.2 131.6 %reduce-scatter.5.cloned.1.call-start = ((), (), s32[]{:S(2)}) async-start(), calls=%async_computation.12 | async-start | bytes 7864320 | tf_op jit(solution)/shard_map/reduce_scatter | solution.py:51
  1069.9 265.9 %reduce-scatter.9.cloned.1.call-start = ((), (), s32[]{:S(2)}) async-start(), calls=%async_computation.14 | async-start | bytes 20971520 | tf_op jit(solution)/shard_map/reduce_scatter | solution.py:51
  1090.6 30.1 %copy-start.1 = (bf16[4,128,2048]{2,1,0:T(8,128)(2,1)S(1)}, bf16[4,128,2048]{2,1,0:T(8,128)(2,1)}, u32[]{:S(2)}) copy-start(bf16[4,128,2048]{2,1,0:T(8,128)(2,1)} %param.20) | copy-start | bytes 6291460
  1090.6 30.1 %copy-start.30 = (f32[2048,1]{0,1:T(1,128)S(1)}, f32[2048,1]{0,1:T(1,128)}, u32[]{:S(2)}) copy-start(f32[2048,1]{0,1:T(1,128)} %copy-done.29) | copy-start | bytes 24580
  1090.6 30.1 %copy-start.32 = (f32[512]{0:T(512)S(1)}, f32[512]{0:T(512)}, u32[]{:S(2)}) copy-start(f32[512]{0:T(512)} %copy-done.31) | copy-start | bytes 6148
  1090.6 458.4 %all-reduce.17.cloned.1.call-start = ((), (), s32[]{:S(2)}) async-start(), calls=%async_computation.16 | async-start | bytes 16781312 | tf_op jit(solution)/shard_map/psum | solution.py:57
  1365.9 14.1 all-to-all-start
  (37 other events, 201.3 us)
Sparse Core Ops, SparseCore 0:
  52.8 297.2 all-gather.3
  371.7 113.7 all-gather.5
  535.5 90.8 all-reduce.8
  659.5 58.5 all-reduce.10
  720.3 92.5 all-reduce.12
  828.9 117.8 all-gather.7
  949.3 26.5 reduce-scatter.6
  978.4 80.0 reduce-scatter.10
  1061.4 59.3 all-reduce.14
  1123.1 62.5 reduce-scatter.4
  1188.4 147.4 reduce-scatter.8
  1361.5 187.5 all-reduce.16
where the time goes:
time: 1600 us; the launch traced here: 1590 us
  waiting for transfers between devices  1020 us (64%)
  matrix products  257 us (16%)
  local copies, waits for them, and re-layouts  170 us (11%)
  other arithmetic  77.2 us (5%)
  blocking collectives  35.6 us (2%)
  between operations  16 us (1%)
    all_gather x1, waiting for transfers between devices, gather_turned(): filled = lax.all_gather(both, axis, axis=0, tiled=True)  295 us
    reduce_scatter x2, waiting for transfers between devices, in_one_piece(): filled = lax.psum_scatter(both, axis, scatter_dimension=dim, tiled=True)  190 us
    psum x1, waiting for transfers between devices, packed_total(): subtotal = lax.psum(vector, axis)  163 us
    all_gather x2, waiting for transfers between devices, sent_together(): lax.all_gather(both, axis, axis=dim, tiled=True)  131 us
    psum x1, waiting for transfers between devices, per_device(): grad_ffn_in = lax.psum(ffn_in_part, 'tensor')  94.8 us
    psum x1, waiting for transfers between devices, per_device(): attn_out = lax.psum(matmul_low(attended, o_full), 'tensor')  80.5 us
    unnamed x121, local copies, waits for them, and re-layouts  51.5 us
    psum x1, waiting for transfers between devices, per_device(): lax.psum(matmul_low(hidden, down_full).astype(jnp.bfloat16), 'tensor')  39.7 us
  transfers between devices with their start and end apart: 13, of which 11 were waited for; matrix products, arithmetic and copies ran while one was open for 17% of the time, Pallas kernels for 0%

commit v1 on v0

v1 whole, which is shorter than its diff:
```python
import functools

import jax
import jax.numpy as jnp
from jax import lax
from jax.experimental import pallas as pl
from jax.experimental.pallas import tpu as pltpu
from jax.sharding import PartitionSpec as P

HEAD_DIM = 64
PIECE = 256
NORM_EPS = 1e-05
ROPE_BASE = 130000.0
MASK_FILL = -1e30
BF = jnp.bfloat16
F32 = jnp.float32
ANY = pl.BlockSpec(memory_space=pl.ANY)
VM = pl.BlockSpec(memory_space=pltpu.VMEM)
DMA = pltpu.SemaphoreType.DMA
VMEM_LIMIT = 60 * 1024 * 1024
MODEL = 2048
BLOCK = 128
MESH_ID = pl.DeviceIdType.MESH


class Place:
    def __init__(self):
        self.s = lax.axis_index("shard")
        self.k = lax.axis_index("context")
        self.x = lax.axis_index("tensor")
        self.yl = self.s // 2
        self.c = self.s % 2
        self.y = (self.k // 4) * 2 + self.yl
        self.z = self.k % 4

    def dev(self, dx=0, dy=0, dz=0, core=None):
        x = (self.x + dx + 4) % 4
        y = (self.y + dy + 4) % 4
        z = (self.z + dz + 4) % 4
        c = self.c if core is None else core
        return {"shard": (y % 2) * 2 + c, "context": (y // 2) * 4 + z, "tensor": x}

    def member(self, k):
        return {"shard": self.s, "context": k, "tensor": self.x}

    def sib(self):
        return self.dev(core=1 - self.c)


def remote(src, dst, send_sem, recv_sem, device):
    return pltpu.make_async_remote_copy(
        src_ref=src,
        dst_ref=dst,
        send_sem=send_sem,
        recv_sem=recv_sem,
        device_id=device,
        device_id_type=MESH_ID,
    )


def greet(devices):
    barrier = pltpu.get_barrier_semaphore()
    for d in devices:
        pl.semaphore_signal(barrier, inc=1, device_id=d, device_id_type=MESH_ID)
    pl.semaphore_wait(barrier, len(devices))


def params(collective_id=None):
    if collective_id is None:
        return pltpu.CompilerParams(vmem_limit_bytes=VMEM_LIMIT)
    return pltpu.CompilerParams(
        vmem_limit_bytes=VMEM_LIMIT, collective_id=collective_id, has_side_effects=True
    )


def tiles(v):
    return v.reshape(*v.shape[:-2], v.shape[-2] // 8, 8, v.shape[-1])


def rows_of(v):
    return v.reshape(*v.shape[:-3], v.shape[-3] * 8, v.shape[-1])


def context_peers(p):
    return [p.member((p.k + d) % 8) for d in range(1, 8)]


def swap_halves(v):
    width = v.shape[1]
    lane = lax.broadcasted_iota(jnp.int32, v.shape, 1) % HEAD_DIM
    return jnp.where(
        lane < HEAD_DIM // 2,
        pltpu.roll(v, width - HEAD_DIM // 2, 1),
        pltpu.roll(v, HEAD_DIM // 2, 1),
    )


WEIGHTS = (
    (256, "row", 0, 0),
    (256, "row", 0, 256),
    (256, "row", 0, 512),
    (256, "col", 1, 0),
    (1024, "row", 2, 0),
    (1024, "row", 2, 1024),
    (1024, "col", 3, 0),
)


def start_kernel(
    x_ref,
    cot_ref,
    wq,
    wk,
    wv,
    wo,
    wg,
    wu,
    wd,
    gain_ref,
    meta_ref,
    cos_ref,
    sin_ref,
    wqkv_o,
    wo_o,
    wgu_o,
    wd_o,
    gains_o,
    meta_o,
    cot_o,
    attn_in_o,
    qkv_o,
    x_all,
    qkv_send,
    y_send,
    y_recv,
    z_send,
    z_recv,
    sib_send,
    sib_recv,
    loc,
    misc_send,
    misc_recv,
    gain_send,
    gain_recv,
    a2a_send,
    a2a_recv,
):
    p = Place()
    srcs = (wq, wk, wv, wo, wg, wu, wd)
    dsts = (wqkv_o, wo_o, wgu_o, wd_o)
    qa = 2 * (p.z % 2)

    def src_part(w, half, quarter):
        size, kind, _, _ = WEIGHTS[w]
        if kind == "row":
            rows = pl.ds(0, 64) if quarter is None else pl.ds(quarter * 16, 16)
            return srcs[w].at[rows, :, pl.ds(half * size, size)]
        size = size // 8
        if quarter is None:
            return srcs[w].at[pl.ds(half * size, size)]
        return srcs[w].at[pl.ds(half * size + quarter * (size // 4), size // 4)]

    def dst_part(w, block, quarter):
        size, kind, d, off = WEIGHTS[w]
        if kind == "row":
            rows = (
                pl.ds(block * 64, 64)
                if quarter is None
                else pl.ds(block * 64 + quarter * 16, 16)
            )
            return dsts[d].at[rows, :, pl.ds(off, size)]
        size = size // 8
        cols = pl.ds(block * 512, 512)
        if quarter is None:
            return dsts[d].at[:, :, cols]
        return dsts[d].at[pl.ds(quarter * (size // 4), size // 4), :, cols]

    def y_copy(w, side, core, block, target_half):
        quarter = qa + side
        return remote(
            src_part(w, target_half, quarter),
            dst_part(w, block, quarter),
            y_send.at[w, side, core],
            y_recv.at[w, side, p.c],
            p.dev(dy=-1 if side == 0 else 1, core=core),
        )

    def y_arrival(w, side, core):
        quarter = qa + side
        here = dst_part(w, (1 - p.yl) * 2 + core, quarter)
        return remote(
            here,
            here,
            y_send.at[w, side, core],
            y_recv.at[w, side, core],
            p.dev(dy=1 if side == 0 else -1, core=core),
        )

    def z_copy(w, side, core):
        here = dst_part(w, (1 - p.yl) * 2 + core, qa + side)
        return remote(
            here,
            here,
            z_send.at[w, side, core],
            z_recv.at[w, side, core],
            p.dev(dz=-1 if side == 0 else 1),
        )

    def z_arrival(w, side, core):
        here = dst_part(w, (1 - p.yl) * 2 + core, 2 - qa + side)
        return remote(
            here,
            here,
            z_send.at[w, side, core],
            z_recv.at[w, side, core],
            p.dev(dz=1 if side == 0 else -1),
        )

    def sib_copy(w):
        return remote(
            src_part(w, 1 - p.c, None),
            dst_part(w, p.s, None),
            sib_send.at[w],
            sib_recv.at[w],
            p.sib(),
        )

    def sib_arrival(w):
        here = dst_part(w, p.yl * 2 + 1 - p.c, None)
        return remote(here, here, sib_send.at[w], sib_recv.at[w], p.sib())

    def own_copy(w):
        return pltpu.make_async_copy(src_part(w, p.c, None), dst_part(w, p.s, None), loc.at[w])

    greet(
        [p.sib()]
        + [p.dev(dy=dy, core=core) for dy in (-1, 1) for core in (0, 1)]
        + context_peers(p)
    )

    def start_y(ws):
        for w in ws:
            for core in (0, 1):
                for side in (0, 1):
                    y_copy(w, side, core, p.s, core).start()

    gain_targets = [p.sib()] + [p.dev(dy=dy, core=core) for dy, core in ((1, 0), (1, 1))]
    gain_copies = [
        remote(gain_ref, gains_o.at[p.s], gain_send.at[i], gain_recv.at[i if i == 0 else 1 + p.c], d)
        for i, d in enumerate(gain_targets)
    ]
    for g in gain_copies:
        g.start()
    x_own = pltpu.make_async_copy(x_ref, x_all.at[:, 0], loc.at[7])
    x_own.start()
    x_out = remote(x_ref, x_all.at[:, 1], misc_send.at[0], misc_recv.at[0], p.sib())
    x_out.start()
    start_y((0, 1, 2))
    for w in (0, 1, 2):
        sib_copy(w).start()
        own_copy(w).start()
    gain_own = pltpu.make_async_copy(gain_ref, gains_o.at[p.s], loc.at[8])
    gain_own.start()
    meta_own = pltpu.make_async_copy(meta_ref, meta_o.at[p.c], loc.at[9])
    meta_own.start()
    meta_out = remote(meta_ref, meta_o.at[p.c], misc_send.at[1], misc_recv.at[1], p.sib())
    meta_out.start()
    cot_own = pltpu.make_async_copy(cot_ref, cot_o.at[:, 0], loc.at[10])
    cot_own.start()
    cot_out = remote(cot_ref, cot_o.at[:, 1], misc_send.at[2], misc_recv.at[2], p.sib())

    gain_own.wait()
    for i in range(3):
        block = p.yl * 2 + 1 - p.c if i == 0 else (1 - p.yl) * 2 + (i - 1)
        here = gains_o.at[block]
        remote(here, here, gain_send.at[i], gain_recv.at[i], p.sib()).wait_recv()
    x_own.wait()
    x_out.wait_recv()
    gain = jnp.concatenate([gains_o[b, 0:1, :] for b in range(4)], axis=1)

    def norm_step(i, carry):
        v = x_all[i // 2, i % 2].astype(F32).reshape(BLOCK, MODEL)
        r = lax.rsqrt(jnp.mean(v * v, axis=1, keepdims=True) + NORM_EPS)
        attn_in_o[i // 2, pl.ds((i % 2) * BLOCK, BLOCK), :] = (v * r * gain).astype(BF)
        return carry

    lax.fori_loop(0, 8, norm_step, 0)

    def pass_on(ws):
        for w in ws:
            for side in (0, 1):
                for core in (0, 1):
                    y_arrival(w, side, core).wait_recv()
                    z_copy(w, side, core).start()

    pass_on((0, 1, 2))
    start_y((3, 4, 5, 6))
    for w in (3, 4, 5, 6):
        sib_copy(w).start()
        own_copy(w).start()
    cot_out.start()
    for w in (0, 1, 2):
        for side in (0, 1):
            for core in (0, 1):
                z_arrival(w, side, core).wait_recv()
        sib_arrival(w).wait_recv()
        own_copy(w).wait()

    def send_block(j, q):
        other = p.c if q == 0 else 1 - p.c
        k = j * 2 + other
        slot = j * 2 + q
        return (
            k,
            remote(
                qkv_send.at[slot],
                qkv_o.at[p.k],
                a2a_send.at[slot],
                a2a_recv.at[p.k],
                p.member(k),
            ),
            pltpu.make_async_copy(qkv_send.at[slot], qkv_o.at[p.k], a2a_send.at[slot]),
        )

    def qkv_step(j, carry):
        a = attn_in_o[j]
        for part in range(3):
            cols = pl.ds(part * 256, 256)
            w = wqkv_o[:, :, cols].reshape(MODEL, 256)
            v = jnp.dot(a, w, preferred_element_type=F32)
            if part < 2:
                v = v * cos_ref[...] + swap_halves(v) * sin_ref[...]
            v = v.reshape(32, 8, 256).astype(BF)
            qkv_send[j * 2, :, :, cols] = v[:16]
            qkv_send[j * 2 + 1, :, :, cols] = v[16:]
        for q in (0, 1):
            k, out, here = send_block(j, q)

            @pl.when(k != p.k)
            def _():
                out.start()

            @pl.when(k == p.k)
            def _():
                here.start()

        return carry

    lax.fori_loop(0, 4, qkv_step, 0)
    pass_on((3, 4, 5, 6))
    for w in (3, 4, 5, 6):
        for side in (0, 1):
            for core in (0, 1):
                z_arrival(w, side, core).wait_recv()
        sib_arrival(w).wait_recv()
        own_copy(w).wait()
    for w in range(7):
        sib_copy(w).wait_send()
        for side in (0, 1):
            for core in (0, 1):
                y_copy(w, side, core, p.s, core).wait_send()
                z_copy(w, side, core).wait_send()
    x_out.wait_send()
    meta_own.wait()
    meta_out.wait_send()
    here = meta_o.at[1 - p.c]
    remote(here, here, misc_send.at[1], misc_recv.at[1], p.sib()).wait_recv()
    cot_own.wait()
    cot_out.wait()
    for g in gain_copies:
        g.wait_send()
    for j in range(4):
        for q in (0, 1):
            k, out, here = send_block(j, q)

            @pl.when(k != p.k)
            def _():
                out.wait_send()

            @pl.when(k == p.k)
            def _():
                here.wait()

    for i in range(8):

        @pl.when(i != p.k)
        def _():
            here = qkv_o.at[i]
            remote(here, here, a2a_send.at[i], a2a_recv.at[i], p.member(i)).wait_recv()


def start_call(x, cot, weights, gains, meta, cos_t, sin_t):
    shapes = (
        jax.ShapeDtypeStruct((256, 8, 768), BF),
        jax.ShapeDtypeStruct((32, 8, 2048), BF),
        jax.ShapeDtypeStruct((256, 8, 2048), BF),
        jax.ShapeDtypeStruct((128, 8, 2048), BF),
        jax.ShapeDtypeStruct((4, 8, 512), F32),
        jax.ShapeDtypeStruct((2, 8, 1024), jnp.int32),
        jax.ShapeDtypeStruct((4, 2, 16, 8, MODEL), BF),
        jax.ShapeDtypeStruct((4, 256, MODEL), BF),
        jax.ShapeDtypeStruct((8, 16, 8, 768), BF),
    )
    return pl.pallas_call(
        start_kernel,
        out_shape=shapes,
        in_specs=[ANY] * 9 + [VM, ANY, VM, VM],
        out_specs=[VM, ANY, ANY, ANY, VM, ANY, ANY, VM, ANY],
        scratch_shapes=[
            pltpu.VMEM((4, 2, 16, 8, MODEL), BF),
            pltpu.VMEM((8, 16, 8, 768), BF),
            DMA((7, 2, 2)),
            DMA((7, 2, 2)),
            DMA((7, 2, 2)),
            DMA((7, 2, 2)),
            DMA((7,)),
            DMA((7,)),
            DMA((11,)),
            DMA((3,)),
            DMA((3,)),
            DMA((3,)),
            DMA((3,)),
            DMA((8,)),
            DMA((8,)),
        ],
        compiler_params=params(1),
    )(tiles(x), tiles(cot), *[tiles(w) for w in weights], gains, meta, cos_t, sin_t)


def bias_rows(qb, rows, prow, vrow, pcol):
    i = qb * rows + lax.broadcasted_iota(jnp.int32, (rows, 1024), 0)
    j = lax.broadcasted_iota(jnp.int32, (rows, 1024), 1)
    same = (pcol >= 0) & (pcol == prow)
    ok = ((j <= i) | same) & ((vrow > 0) | (i == j))
    return jnp.where(ok, 0.0, MASK_FILL)


def attend_kernel(
    qkv, info, pcol, out_o, lse_o, o_send, a2a_send, a2a_recv
):
    p = Place()
    greet(context_peers(p))
    rows = 256

    def sends(i):
        return (
            remote(o_send.at[i], out_o.at[p.k], a2a_send.at[i], a2a_recv.at[p.k], p.member(i)),
            pltpu.make_async_copy(o_send.at[i], out_o.at[p.k], a2a_send.at[i]),
        )

    def step(qb, carry):
        at = pl.ds(pl.multiple_of(qb * rows, rows), rows)
        bias = bias_rows(qb, rows, info[0:1, :], info[1:2, :], pcol[at, 0:1])
        lane = lax.broadcasted_iota(jnp.int32, (rows, 128), 1)
        totals = jnp.zeros((rows, 128), F32)
        outs = []
        for h in range(4):
            q = qkv[at, pl.ds(h * 64, 64)]
            k = qkv[:, pl.ds(256 + h * 64, 64)]
            v = qkv[:, pl.ds(512 + h * 64, 64)]
            sc = lax.dot_general(q, k, (((1,), (1,)), ((), ())), preferred_element_type=F32)
            sc = sc * (HEAD_DIM**-0.5) + bias
            top = jnp.max(sc, axis=1, keepdims=True)
            e = jnp.exp(sc - top)
            total = jnp.sum(e, axis=1, keepdims=True)
            prob = (e * (1.0 / total)).astype(BF)
            totals = jnp.where(lane == h, top + jnp.log(total), totals)
            outs.append(jnp.dot(prob, v, preferred_element_type=F32))
        lse_o[at, :] = totals
        o = jnp.concatenate(outs, axis=1).reshape(32, 8, 256).astype(BF)
        for half in (0, 1):
            i = qb * 2 + half
            o_send[i] = o[half * 16 : (half + 1) * 16]
            out, here = sends(i)

            @pl.when(i != p.k)
            def _():
                out.start()

            @pl.when(i == p.k)
            def _():
                here.start()

        return carry

    lax.fori_loop(0, 4, step, 0)
    for i in range(8):
        out, here = sends(i)

        @pl.when(i != p.k)
        def _():
            out.wait_send()
            spot = out_o.at[i]
            remote(spot, spot, a2a_send.at[i], a2a_recv.at[i], p.member(i)).wait_recv()

        @pl.when(i == p.k)
        def _():
            here.wait()


def attend_call(qkv, info, pcol):
    return pl.pallas_call(
        attend_kernel,
        out_shape=(
            jax.ShapeDtypeStruct((8, 16, 8, 256), BF),
            jax.ShapeDtypeStruct((1024, 128), F32),
        ),
        in_specs=[VM] * 3,
        out_specs=[ANY, VM],
        scratch_shapes=[pltpu.VMEM((8, 16, 8, 256), BF), DMA((8,)), DMA((8,))],
        compiler_params=params(2),
    )(qkv, info, pcol)


def attend_back_kernel(
    g_ref,
    qkv,
    info,
    pcol,
    lse,
    cos_ref,
    sin_ref,
    out_o,
    g_all,
    d_send,
    dk,
    dv,
    g_send,
    g_recv,
    a2a_send,
    a2a_recv,
):
    p = Place()
    greet(context_peers(p))
    rows = 256

    def g_copy(j, q):
        other = p.c if q == 0 else 1 - p.c
        k = j * 2 + other
        slot = j * 2 + q
        return (
            k,
            remote(g_ref.at[slot], g_all.at[p.k], g_send.at[slot], g_recv.at[p.k], p.member(k)),
            pltpu.make_async_copy(g_ref.at[slot], g_all.at[p.k], g_send.at[slot]),
        )

    for j in range(4):
        for q in (0, 1):
            k, out, here = g_copy(j, q)

            @pl.when(k != p.k)
            def _():
                out.start()

            @pl.when(k == p.k)
            def _():
                here.start()

    dk[...] = jnp.zeros_like(dk)
    dv[...] = jnp.zeros_like(dv)
    for j in range(4):
        for q in (0, 1):
            k, out, here = g_copy(j, q)

            @pl.when(k != p.k)
            def _():
                out.wait_send()

            @pl.when(k == p.k)
            def _():
                here.wait()

    for i in range(8):

        @pl.when(i != p.k)
        def _():
            spot = g_all.at[i]
            remote(spot, spot, g_send.at[i], g_recv.at[i], p.member(i)).wait_recv()

    def sends(i):
        return (
            remote(d_send.at[i], out_o.at[p.k], a2a_send.at[i], a2a_recv.at[p.k], p.member(i)),
            pltpu.make_async_copy(d_send.at[i], out_o.at[p.k], a2a_send.at[i]),
        )

    scale = HEAD_DIM**-0.5

    def step(qb, carry):
        at = pl.ds(pl.multiple_of(qb * rows, rows), rows)
        bias = bias_rows(qb, rows, info[0:1, :], info[1:2, :], pcol[at, 0:1])
        g2 = g_all[pl.ds(qb * 2, 2)].astype(F32).reshape(rows, 256).astype(BF)
        dqs = []
        for h in range(4):
            lanes = pl.ds(h * 64, 64)
            q = qkv[at, lanes]
            k = qkv[:, pl.ds(256 + h * 64, 64)]
            v = qkv[:, pl.ds(512 + h * 64, 64)]
            g = g2[:, h * 64 : (h + 1) * 64]
            sc = lax.dot_general(q, k, (((1,), (1,)), ((), ())), preferred_element_type=F32)
            prob = jnp.exp(sc * scale + bias - lse[at, h : h + 1])
            gp = lax.dot_general(g, v, (((1,), (1,)), ((), ())), preferred_element_type=F32)
            inner = jnp.sum(prob * gp, axis=1, keepdims=True)
            gs = (prob * (gp - inner)).astype(BF)
            dqs.append(jnp.dot(gs, k, preferred_element_type=F32))
            dk[:, lanes] += lax.dot_general(
                gs, q, (((0,), (0,)), ((), ())), preferred_element_type=F32
            )
            dv[:, lanes] += lax.dot_general(
                prob.astype(BF), g, (((0,), (0,)), ((), ())), preferred_element_type=F32
            )
        dq = jnp.concatenate(dqs, axis=1) * scale
        dq = dq * cos_ref[at, :] - swap_halves(dq) * sin_ref[at, :]
        dq = dq.reshape(32, 8, 256).astype(BF)
        d_send[qb * 2, :, :, 0:256] = dq[:16]
        d_send[qb * 2 + 1, :, :, 0:256] = dq[16:]
        return carry

    lax.fori_loop(0, 4, step, 0)

    def finish(i, carry):
        at = pl.ds(pl.multiple_of(i * BLOCK, BLOCK), BLOCK)
        w = dk[at, :] * scale
        w = w * cos_ref[at, :] - swap_halves(w) * sin_ref[at, :]
        d_send[i, :, :, 256:512] = w.reshape(16, 8, 256).astype(BF)
        d_send[i, :, :, 512:768] = dv[at, :].reshape(16, 8, 256).astype(BF)
        out, here = sends(i)

        @pl.when(i != p.k)
        def _():
            out.start()

        @pl.when(i == p.k)
        def _():
            here.start()

        return carry

    lax.fori_loop(0, 8, finish, 0)
    for i in range(8):
        out, here = sends(i)

        @pl.when(i != p.k)
        def _():
            out.wait_send()
            spot = out_o.at[i]
            remote(spot, spot, a2a_send.at[i], a2a_recv.at[i], p.member(i)).wait_recv()

        @pl.when(i == p.k)
        def _():
            here.wait()


def attend_back_call(g, qkv, info, pcol, lse, cos_full, sin_full):
    return pl.pallas_call(
        attend_back_kernel,
        out_shape=jax.ShapeDtypeStruct((8, 16, 8, 768), BF),
        in_specs=[VM] * 7,
        out_specs=ANY,
        scratch_shapes=[
            pltpu.VMEM((8, 16, 8, 256), BF),
            pltpu.VMEM((8, 16, 8, 768), BF),
            pltpu.VMEM((1024, 256), F32),
            pltpu.VMEM((1024, 256), F32),
            DMA((8,)),
            DMA((8,)),
            DMA((8,)),
            DMA((8,)),
        ],
        compiler_params=params(5),
    )(tiles(g), qkv, info, pcol, lse, cos_full, sin_full)


RS_SCRATCH = [
    pltpu.VMEM((4, BLOCK, MODEL), F32),
    pltpu.VMEM((4, BLOCK, MODEL), BF),
    pltpu.VMEM((4, BLOCK, MODEL), BF),
    pltpu.VMEM((3, BLOCK, MODEL), BF),
    pltpu.VMEM((3, BLOCK, MODEL), BF),
    DMA((4,)),
    DMA((4,)),
    DMA((4,)),
    DMA((4,)),
]
AG_SCRATCH = [DMA((8,)), DMA((8,))]


def x_peers(p):
    return [p.sib(), p.dev(dx=1), p.dev(dx=-1)]


def reduce_scatter(p, lhs, rhs, transposed, scratch):
    acc, sib_out, sib_in, x_out, x_in, s_send, s_recv, x_send, x_recv = scratch
    tile = 256
    half = BLOCK // 2

    def sib_copy(r):
        return remote(sib_out.at[r], sib_in.at[r], s_send.at[r], s_recv.at[r], p.sib())

    def product(r):
        j = (p.x + r) % 4

        def step(n, carry):
            a = lhs[j]
            cols = pl.ds(pl.multiple_of(n * tile, tile), tile)
            if transposed:
                v = lax.dot_general(
                    a, rhs[cols, :], (((1,), (1,)), ((), ())), preferred_element_type=F32
                )
            else:
                v = jnp.dot(a, rhs[:, cols], preferred_element_type=F32)
            acc[r, :, cols] = v[:BLOCK]
            sib_out[r, :, cols] = v[BLOCK:].astype(BF)
            return carry

        lax.fori_loop(0, MODEL // tile, step, 0)
        sib_copy(r).start()

    far_right = remote(
        x_out.at[0, pl.ds(0, half)], x_in.at[0, pl.ds(0, half)], x_send.at[0], x_recv.at[0], p.dev(dx=1)
    )
    far_left = remote(
        x_out.at[0, pl.ds(half, half)],
        x_in.at[0, pl.ds(half, half)],
        x_send.at[1],
        x_recv.at[1],
        p.dev(dx=-1),
    )
    right = remote(x_out.at[1], x_in.at[1], x_send.at[2], x_recv.at[2], p.dev(dx=1))
    left = remote(x_out.at[2], x_in.at[2], x_send.at[3], x_recv.at[3], p.dev(dx=-1))
    product(2)
    product(1)
    sib_copy(2).wait_recv()
    x_out[0] = (acc[2] + sib_in[2].astype(F32)).astype(BF)
    far_right.start()
    far_left.start()
    product(3)
    sib_copy(1).wait_recv()
    far_right.wait_recv()
    x_out[1, 0:half] = (
        acc[1, 0:half] + sib_in[1, 0:half].astype(F32) + x_in[0, 0:half].astype(F32)
    ).astype(BF)
    x_out[1, half:] = (acc[1, half:] + sib_in[1, half:].astype(F32)).astype(BF)
    right.start()
    sib_copy(3).wait_recv()
    far_left.wait_recv()
    x_out[2, 0:half] = (acc[3, 0:half] + sib_in[3, 0:half].astype(F32)).astype(BF)
    x_out[2, half:] = (
        acc[3, half:] + sib_in[3, half:].astype(F32) + x_in[0, half:].astype(F32)
    ).astype(BF)
    left.start()
    product(0)
    sib_copy(0).wait_recv()
    right.wait_recv()
    left.wait_recv()
    total = acc[0] + sib_in[0].astype(F32) + x_in[1].astype(F32) + x_in[2].astype(F32)
    for r in range(4):
        sib_copy(r).wait_send()
    for c in (far_right, far_left, right, left):
        c.wait_send()
    return total


def all_gather(p, out, sems, both):
    send, recv = sems
    half = BLOCK // 2
    me, right, left, far = p.x, (p.x + 1) % 4, (p.x + 3) % 4, (p.x + 2) % 4

    def copy(n, j, rows, d):
        src = out.at[j, 0] if rows is None else out.at[j, 0, rows]
        return remote(src, src, send.at[n], recv.at[n], d)

    top, low = pl.ds(0, half), pl.ds(half, half)
    sent = []

    def go(c):
        c.start()
        sent.append(c)

    def sib_copy(n, j):
        return remote(out.at[j, 0], out.at[j, 1], send.at[n], recv.at[n], p.sib())

    go(copy(0, me, None, p.dev(dx=1)))
    go(copy(1, me, None, p.dev(dx=-1)))
    if both:
        go(sib_copy(4, me))
    copy(0, left, None, p.dev(dx=-1)).wait_recv()
    go(copy(2, left, top, p.dev(dx=1)))
    if both:
        go(sib_copy(5, left))
    copy(1, right, None, p.dev(dx=1)).wait_recv()
    go(copy(3, right, low, p.dev(dx=-1)))
    if both:
        go(sib_copy(6, right))
    copy(2, far, top, p.dev(dx=-1)).wait_recv()
    copy(3, far, low, p.dev(dx=1)).wait_recv()
    if both:
        go(sib_copy(7, far))
        for n, j in ((4, me), (5, left), (6, right), (7, far)):
            sib_copy(n, j).wait_recv()
    for c in sent:
        c.wait_send()


def rms(v):
    return lax.rsqrt(jnp.mean(v * v, axis=1, keepdims=True) + NORM_EPS)


def full_row(gains, row):
    return jnp.concatenate([gains[b, row : row + 1, :] for b in range(4)], axis=1)


def norm_back(grad, normed, gain, inv):
    w = grad * gain
    return inv * (w - normed * jnp.mean(w * normed, axis=1, keepdims=True))


def out_proj_kernel(lhs, rhs, x_own, keep, gains, ffn_in_o, resid_o, stat_o, *scratch):
    p = Place()
    greet(x_peers(p))
    attn_out = reduce_scatter(p, lhs, rhs, False, scratch[: len(RS_SCRATCH)])
    stat_o[...] = jnp.full((8, 128), jnp.sum(keep[:, 0:1] * attn_out * attn_out), F32)
    resid = x_own[...].astype(F32) + attn_out
    resid_o[...] = resid
    ffn_in_o[p.x, 0] = (resid * rms(resid) * full_row(gains, 1)).astype(BF)
    all_gather(p, ffn_in_o, scratch[len(RS_SCRATCH) :], True)


def out_proj_call(lhs, rhs, x_own, keep, gains):
    return pl.pallas_call(
        out_proj_kernel,
        out_shape=(
            jax.ShapeDtypeStruct((4, 2, BLOCK, MODEL), BF),
            jax.ShapeDtypeStruct((BLOCK, MODEL), F32),
            jax.ShapeDtypeStruct((8, 128), F32),
        ),
        in_specs=[VM] * 5,
        out_specs=[VM] * 3,
        scratch_shapes=RS_SCRATCH + AG_SCRATCH,
        compiler_params=params(3),
    )(lhs, rhs, x_own, keep, gains)


def ffn_out_kernel(lhs, rhs, resid, keep, out_o, stat_o, *scratch):
    p = Place()
    greet(x_peers(p))
    ffn_out = reduce_scatter(p, lhs, rhs, False, scratch[: len(RS_SCRATCH)])
    final = resid[...] + ffn_out
    k = keep[:, 0:1]
    stat_o[0] = jnp.full((8, 128), jnp.sum(k * ffn_out * ffn_out), F32)
    stat_o[1] = jnp.full((8, 128), jnp.sum(k * final * final), F32)
    out_o[p.x, 0] = final.astype(BF)
    all_gather(p, out_o, scratch[len(RS_SCRATCH) :], False)


def ffn_out_call(lhs, rhs, resid, keep):
    return pl.pallas_call(
        ffn_out_kernel,
        out_shape=(
            jax.ShapeDtypeStruct((4, 1, BLOCK, MODEL), BF),
            jax.ShapeDtypeStruct((2, 8, 128), F32),
        ),
        in_specs=[VM] * 4,
        out_specs=[VM] * 2,
        scratch_shapes=RS_SCRATCH + AG_SCRATCH,
        compiler_params=params(8),
    )(lhs, rhs, resid, keep)


def ffn_back_kernel(lhs, rhs, resid_ref, cot_own, gains, grad_o, resid_grad_o, gain_o, *scratch):
    p = Place()
    greet(x_peers(p))
    g = reduce_scatter(p, lhs, rhs, True, scratch[: len(RS_SCRATCH)])
    resid = resid_ref[...]
    inv = rms(resid)
    normed = resid * inv
    gain_o[...] = jnp.broadcast_to(jnp.sum(g * normed, axis=0, keepdims=True), (8, MODEL))
    grad_resid = cot_own[...].astype(F32) + norm_back(g, normed, full_row(gains, 1), inv)
    resid_grad_o[...] = grad_resid
    grad_o[p.x, 0] = grad_resid.astype(BF)
    all_gather(p, grad_o, scratch[len(RS_SCRATCH) :], True)


def ffn_back_call(lhs, rhs, resid, cot_own, gains):
    return pl.pallas_call(
        ffn_back_kernel,
        out_shape=(
            jax.ShapeDtypeStruct((4, 2, BLOCK, MODEL), BF),
            jax.ShapeDtypeStruct((BLOCK, MODEL), F32),
            jax.ShapeDtypeStruct((8, MODEL), F32),
        ),
        in_specs=[VM] * 5,
        out_specs=[VM] * 3,
        scratch_shapes=RS_SCRATCH + AG_SCRATCH,
        compiler_params=params(4),
    )(lhs, rhs, resid, cot_own, gains)


def attn_in_back_kernel(lhs, rhs, x_own, grad_resid, gains, out_o, gain_o, *scratch):
    p = Place()
    greet(x_peers(p))
    g = reduce_scatter(p, lhs, rhs, True, scratch[: len(RS_SCRATCH)])
    v = x_own[...].astype(F32)
    inv = rms(v)
    normed = v * inv
    gain_o[...] = jnp.broadcast_to(jnp.sum(g * normed, axis=0, keepdims=True), (8, MODEL))
    grad_in = grad_resid[...] + norm_back(g, normed, full_row(gains, 0), inv)
    out_o[p.x, 0] = grad_in.astype(BF)
    all_gather(p, out_o, scratch[len(RS_SCRATCH) :], False)


def attn_in_back_call(lhs, rhs, x_own, grad_resid, gains):
    return pl.pallas_call(
        attn_in_back_kernel,
        out_shape=(
            jax.ShapeDtypeStruct((4, 1, BLOCK, MODEL), BF),
            jax.ShapeDtypeStruct((8, MODEL), F32),
        ),
        in_specs=[VM] * 5,
        out_specs=[VM] * 2,
        scratch_shapes=RS_SCRATCH + AG_SCRATCH,
        compiler_params=params(6),
    )(lhs, rhs, x_own, grad_resid, gains)


UNITS = (
    (128, 512, 3, "col"),
    (64, 2048, 2, "row"),
    (32, 512, 1, "col"),
    (64, 768, 0, "row"),
)


def sum_kernel(*refs):
    nu = len(UNITS)
    srcs = refs[:4]
    outs = refs[4 : 4 + nu]
    at = 4 + nu
    own, yin, zout, zin, yhin = (refs[at + i * nu : at + (i + 1) * nu] for i in range(5))
    at += 5 * nu
    loc, send, recv = refs[at : at + 3]
    p = Place()
    greet(
        [p.sib(), p.dev(dy=1), p.dev(dy=-1), p.dev(dy=2), p.dev(dz=1), p.dev(dz=-1)]
    )

    def block_rows(u, block, rows):
        r, cols, src, kind = UNITS[u]
        if kind == "row":
            return srcs[src].at[pl.ds(block * r + rows[0], rows[1])]
        return srcs[src].at[pl.ds(rows[0], rows[1]), :, pl.ds(block * cols, cols)]

    def unit(u):
        rows, cols, _, _ = UNITS[u]
        part = rows // 8
        half = rows // 2
        waits = []

        def cp(n, src, dst, d):
            return remote(src, dst, send.at[u, n], recv.at[u, n], d)

        for core in (0, 1):
            for h in (0, 1):
                c = cp(
                    core * 2 + h,
                    block_rows(u, (1 - p.yl) * 2 + core, (h * half, half)),
                    yin[u].at[core, h],
                    p.dev(dy=1 if h == 0 else -1),
                )
                c.start()
                waits.append(c)
        local = []
        for core in (0, 1):
            for h in (0, 1):
                c = pltpu.make_async_copy(
                    block_rows(u, p.yl * 2 + core, (h * half, half)),
                    own[u].at[core, h],
                    loc.at[u, core * 2 + h],
                )
                c.start()
                local.append(c)
        yield
        for core in (0, 1):
            for h in (0, 1):
                local[core * 2 + h].wait()
                waits[core * 2 + h].wait_recv()
                own[u][core, h] = (
                    own[u][core, h].astype(F32) + yin[u][core, h].astype(F32)
                ).astype(BF)
        me, zr, zl, zf = p.z, (p.z + 1) % 4, (p.z + 3) % 4, (p.z + 2) % 4

        def chunk(ref, core, h, zc):
            return ref.at[core, h, pl.ds(zc * part, part)]

        far = []
        for core in (0, 1):
            for h in (0, 1):
                c = cp(
                    4 + core * 2 + h,
                    chunk(own[u], core, h, zf),
                    zin[u].at[0, core, h],
                    p.dev(dz=1 if h == 0 else -1),
                )
                c.start()
                far.append(c)
        yield
        near = []
        for side, zc in ((0, zr), (1, zl)):
            for core in (0, 1):
                for h in (0, 1):
                    v = own[u][core, h, pl.ds(zc * part, part)].astype(F32)
                    if h == side:
                        far[core * 2 + h].wait_recv()
                        v = v + zin[u][0, core, h].astype(F32)
                    zout[u][side, core, h] = v.astype(BF)
            c = cp(8 + side, zout[u].at[side], zin[u].at[1 + side], p.dev(dz=1 if side == 0 else -1))
            c.start()
            near.append(c)
        yield
        for c in near:
            c.wait_recv()
        for c in near:
            c.wait_send()
        for core in (0, 1):
            for h in (0, 1):
                v = own[u][core, h, pl.ds(me * part, part)].astype(F32)
                v = v + zin[u][1, core, h].astype(F32) + zin[u][2, core, h].astype(F32)
                zout[u][0, core, h] = v.astype(BF)
        yh = cp(10, zout[u].at[0], yhin[u], p.dev(dy=2))
        yh.start()
        for c in far:
            c.wait_send()
        yield
        yh.wait_recv()
        for core in (0, 1):
            for h in (0, 1):
                own[u][core, h, pl.ds(me * part, part)] = (
                    zout[u][0, core, h].astype(F32) + yhin[u][core, h].astype(F32)
                ).astype(BF)
        first = []
        for core in (0, 1):
            for h in (0, 1):
                for side in (0, 1):
                    here = chunk(own[u], core, h, me)
                    c = cp(
                        11 + core * 4 + h * 2 + side, here, here, p.dev(dz=1 if side == 0 else -1)
                    )
                    c.start()
                    first.append(c)
        yield
        second = []
        for core in (0, 1):
            for h in (0, 1):
                for side, zc in ((0, zl), (1, zr)):
                    here = chunk(own[u], core, h, zc)
                    n = 11 + core * 4 + h * 2 + side
                    cp(n, here, here, p.dev(dz=-1 if side == 0 else 1)).wait_recv()
                    if h == side:
                        c = cp(19 + core * 2 + h, here, here, p.dev(dz=1 if side == 0 else -1))
                        c.start()
                        second.append(c)
        yield
        for core in (0, 1):
            for h in (0, 1):
                here = chunk(own[u], core, h, zf)
                cp(19 + core * 2 + h, here, here, p.dev(dz=-1 if h == 0 else 1)).wait_recv()
        for c in first + second + waits + [yh]:
            c.wait_send()
        c = cp(23, own[u].at[1 - p.c], outs[u].at[1], p.sib())
        c.start()
        o = pltpu.make_async_copy(own[u].at[p.c], outs[u].at[0], loc.at[u, 4])
        o.start()
        yield
        c.wait()
        o.wait()

    todo = [unit(u) for u in range(nu)]
    alive = [True] * nu
    step = 0
    while any(alive):
        for u in range(nu):
            if alive[u] and step >= u:
                try:
                    next(todo[u])
                except StopIteration:
                    alive[u] = False
        step += 1


def sum_call(dqkv, do, dgu, dd):
    def bufs(shape):
        return [pltpu.VMEM(shape(r, c), BF) for r, c, _, _ in UNITS]

    return pl.pallas_call(
        sum_kernel,
        out_shape=tuple(
            jax.ShapeDtypeStruct((2, 2, r // 2, 8, c), BF) for r, c, _, _ in UNITS
        ),
        in_specs=[ANY] * 4,
        out_specs=[ANY] * len(UNITS),
        scratch_shapes=bufs(lambda r, c: (2, 2, r // 2, 8, c))
        + bufs(lambda r, c: (2, 2, r // 2, 8, c))
        + bufs(lambda r, c: (2, 2, 2, r // 8, 8, c))
        + bufs(lambda r, c: (3, 2, 2, r // 8, 8, c))
        + bufs(lambda r, c: (2, 2, r // 8, 8, c))
        + [DMA((len(UNITS), 5)), DMA((len(UNITS), 24)), DMA((len(UNITS), 24))],
        compiler_params=params(7),
    )(tiles(dqkv), tiles(do), tiles(dgu), tiles(dd))


def rope_tables(positions, head_size):
    half_dim = head_size // 2
    inv_freq = ROPE_BASE ** (-jnp.arange(half_dim, dtype=jnp.float32) * 2.0 / head_size)
    angles = positions.astype(jnp.float32)[:, None] * inv_freq[None, :]
    cosine, sine = jnp.cos(angles), jnp.sin(angles)
    return jnp.concatenate([cosine, cosine], axis=1), jnp.concatenate([-sine, sine], axis=1)


def piece_index(starts, piece_tags, positions):
    inside = (positions[None, :, None] >= starts[:, None, :]) & (
        positions[None, :, None] < starts[:, None, :] + PIECE
    )
    tagged = jnp.where(inside, piece_tags[:, None, :] + 1, 0)
    return jnp.sum(tagged, axis=2) - 1


def per_device(
    inputs,
    cotangent,
    q_weight,
    k_weight,
    v_weight,
    o_weight,
    gate_weight,
    up_weight,
    down_weight,
    attn_gain,
    ffn_gain,
    piece_starts,
    piece_ids,
    valid_mask,
):
    x_at = lax.axis_index("tensor")
    core = lax.axis_index("shard") % 2
    ctx = lax.axis_index("context")
    positions = jnp.arange(1024, dtype=jnp.int32)
    cos_t, sin_t = rope_tables(positions, HEAD_DIM)
    cos_full, sin_full = jnp.tile(cos_t, (1, 4)), jnp.tile(sin_t, (1, 4))
    cos_own = jnp.tile(lax.dynamic_slice_in_dim(cos_full, ctx * BLOCK, BLOCK, 0), (2, 1))
    sin_own = jnp.tile(lax.dynamic_slice_in_dim(sin_full, ctx * BLOCK, BLOCK, 0), (2, 1))
    meta = jnp.concatenate([piece_index(piece_starts, piece_ids, positions), valid_mask], axis=0)
    gains_own = jnp.concatenate(
        [
            attn_gain.astype(F32)[None],
            ffn_gain.astype(F32)[None],
            jnp.zeros((6, attn_gain.shape[0]), F32),
        ],
        axis=0,
    )
    wqkv, wo, wgu, wd, gains, meta_all, cot_all, attn_in, qkv = start_call(
        inputs,
        cotangent,
        (q_weight, k_weight, v_weight, o_weight, gate_weight, up_weight, down_weight),
        gains_own,
        meta,
        cos_own,
        sin_own,
    )
    seq = lax.dynamic_slice(meta_all, (ctx % 2, 0, 0), (1, 8, 1024))[0]
    piece_row = lax.dynamic_slice_in_dim(seq, ctx // 2, 1, 0)
    valid_row = lax.dynamic_slice_in_dim(seq, 4 + ctx // 2, 1, 0)
    info = jnp.concatenate([piece_row, valid_row, jnp.zeros((6, 1024), jnp.int32)], axis=0)
    pcol = jnp.broadcast_to(piece_row.reshape(1024, 1), (1024, 128))
    wqkv, wo, wgu, wd = rows_of(wqkv), rows_of(wo), rows_of(wgu), rows_of(wd)
    cot_all = rows_of(cot_all)
    qkv = qkv.reshape(1024, 768)
    attended_seq, lse = attend_call(qkv, info, pcol)
    slots = attended_seq.reshape(4, 2, BLOCK, 256)
    attended = jnp.where(core == 0, slots, slots[:, ::-1])
    x_own = lax.dynamic_index_in_dim(inputs, x_at, 0, keepdims=False)
    cot_own = lax.dynamic_index_in_dim(cotangent, x_at, 0, keepdims=False)
    keep_own = lax.dynamic_slice(valid_mask, (x_at, ctx * BLOCK), (1, BLOCK)).astype(F32)
    keep = jnp.broadcast_to(keep_own.reshape(BLOCK, 1), (BLOCK, 128))
    attended = attended.reshape(4, 256, 256)
    ffn_in, resid, stat_attn = out_proj_call(attended, wo, x_own, keep, gains)
    ffn_in = ffn_in.reshape(1024, MODEL)
    cot_rows = cot_all.reshape(1024, MODEL)
    gate_val = jnp.dot(ffn_in, wgu[:, :1024], preferred_element_type=F32)
    up_val = jnp.dot(ffn_in, wgu[:, 1024:], preferred_element_type=F32)
    grad_hidden = jnp.einsum("nd,fd->nf", cot_rows, wd, preferred_element_type=F32)
    gate_sig = jax.nn.sigmoid(gate_val)
    hidden = (gate_val * gate_sig * up_val).astype(BF)
    grad_gate = (grad_hidden * up_val * gate_sig * (1.0 + gate_val * (1.0 - gate_sig))).astype(BF)
    grad_up = (grad_hidden * gate_val * gate_sig).astype(BF)
    grad_gu = jnp.concatenate([grad_gate, grad_up], axis=1)
    grad_attn, grad_resid, ffn_gain_part = ffn_back_call(
        grad_gu.reshape(4, 256, 2048), wgu, resid, cot_own, gains
    )
    grad_attn = grad_attn.reshape(1024, MODEL)
    grad_att = jnp.einsum("nd,cd->nc", grad_attn, wo, preferred_element_type=F32).astype(BF)
    d_seq = attend_back_call(
        grad_att.reshape(8, BLOCK, 256), qkv, info, pcol, lse, cos_full, sin_full
    )
    slots = d_seq.reshape(4, 2, BLOCK, 768)
    dqkv = jnp.where(core == 0, slots, slots[:, ::-1]).reshape(4, 256, 768)
    input_grad, attn_gain_part = attn_in_back_call(dqkv, wqkv, x_own, grad_resid, gains)
    output, stat_ffn = ffn_out_call(hidden.reshape(4, 256, 1024), wd, resid, keep)

    def back(a, b):
        return jnp.einsum("nd,nf->df", a, b, preferred_element_type=F32).astype(BF)

    attn_rows = attn_in.reshape(1024, MODEL)
    dd = back(hidden, cot_rows)
    dgu = back(ffn_in, grad_gu)
    do = back(attended.reshape(1024, 256), grad_attn)
    dw = back(attn_rows, dqkv.reshape(1024, 768))
    sd, sgu, so, sqkv = sum_call(dw, do, dgu, dd)

    def halves(v, rows, cols):
        v = v.reshape(2, rows, cols).astype(F32)
        return jnp.where(core == 0, v, v[::-1])

    sd = halves(sd, 1024, 512).reshape(2048, 512)
    so = halves(so, 256, 512).reshape(512, 512)
    sgu = halves(sgu, 512, 2048)
    gate_grad = jnp.concatenate([sgu[0, :, :1024], sgu[1, :, :1024]], axis=1)
    up_grad = jnp.concatenate([sgu[0, :, 1024:], sgu[1, :, 1024:]], axis=1)
    sqkv = halves(sqkv, 512, 768)
    qkv_grads = [
        jnp.concatenate([sqkv[0, :, i * 256 : (i + 1) * 256], sqkv[1, :, i * 256 : (i + 1) * 256]], axis=1)
        for i in range(3)
    ]
    small = jnp.concatenate(
        [
            attn_gain_part[0],
            ffn_gain_part[0],
            jnp.stack(
                [jnp.sum(keep_own), stat_attn[0, 0], stat_ffn[0, 0, 0], stat_ffn[1, 0, 0]]
            ),
            jnp.zeros((124,), F32),
        ]
    )
    small = lax.psum(small, ("shard", "context", "tensor"))
    stat = small[2 * MODEL : 2 * MODEL + 4]
    branch_rms = jnp.sqrt(stat[1:] / (jnp.maximum(stat[0], 1.0) * MODEL))
    gain_start = (lax.axis_index("shard") * 4 + x_at) * BLOCK
    attn_gain_out = lax.dynamic_slice_in_dim(small, gain_start, BLOCK, 0)
    ffn_gain_out = lax.dynamic_slice_in_dim(small, MODEL + gain_start, BLOCK, 0)
    return (
        output.reshape(4, BLOCK, MODEL),
        input_grad.reshape(4, BLOCK, MODEL),
        *qkv_grads,
        so,
        gate_grad,
        up_grad,
        sd,
        attn_gain_out,
        ffn_gain_out,
        branch_rms,
    )


def solution(mesh):
    return jax.shard_map(
        per_device,
        mesh=mesh,
        in_specs=(
            P("shard", "context", None),
            P("shard", "context", None),
            P("shard", "tensor"),
            P("shard", "tensor"),
            P("shard", "tensor"),
            P("tensor", "shard"),
            P("shard", "tensor"),
            P("shard", "tensor"),
            P("tensor", "shard"),
            P("shard"),
            P("shard"),
            P("shard", None),
            P("shard", None),
            P("shard", None),
        ),
        out_specs=(
            P("shard", "context", None),
            P("shard", "context", None),
            P("shard", "tensor"),
            P("shard", "tensor"),
            P("shard", "tensor"),
            P("tensor", "shard"),
            P("shard", "tensor"),
            P("shard", "tensor"),
            P("tensor", "shard"),
            P(("shard", "tensor")),
            P(("shard", "tensor")),
            P(),
        ),
        check_vma=False,
    )
```

time: 1600 us -> 888 us (0.56)
  the two profiles are of different devices: /device:TPU:1 before, /device:TPU:25 now
where the time goes in v1:
time: 888 us; the launch traced here: 878 us
  Pallas kernels  683 us (77%)
  blocking collectives  69.5 us (8%)
  matrix products  65.4 us (7%)
  other arithmetic  30.9 us (3%)
  local copies, waits for them, and re-layouts  26.6 us (3%)
    pallas_call x1, Pallas kernels, sum_call(): pl.pallas_call(sum_kernel, out_shape=tuple((jax.ShapeDtypeStruct((2, 2, r...  209 us
    pallas_call x1, Pallas kernels, start_call(): pl.pallas_call(start_kernel, out_shape=shapes, in_specs=[ANY] * 9 + [VM,...  179 us
    psum x1, blocking collectives, per_device(): small = lax.psum(small, ('shard', 'context', 'tensor'))  69.5 us
    pallas_call x1, Pallas kernels, ffn_back_call(): pl.pallas_call(ffn_back_kernel, out_shape=(jax.ShapeDtypeStruct((4, 2, BL...  60.3 us
    pallas_call x1, Pallas kernels, out_proj_call(): pl.pallas_call(out_proj_kernel, out_shape=(jax.ShapeDtypeStruct((4, 2, BL...  54.4 us
    pallas_call x1, Pallas kernels, attn_in_back_call(): pl.pallas_call(attn_in_back_kernel, out_shape=(jax.ShapeDtypeStruct((4, 1...  53.7 us
    pallas_call x1, Pallas kernels, attend_back_call(): pl.pallas_call(attend_back_kernel, out_shape=jax.ShapeDtypeStruct((8, 16,...  52.9 us
    pallas_call x1, Pallas kernels, ffn_out_call(): pl.pallas_call(ffn_out_kernel, out_shape=(jax.ShapeDtypeStruct((4, 1, BLO...  49.8 us

profile of v1, /device:TPU:25, one launch (start us, length us, event | category | flops | bytes accessed | tf_op | source)
XLA Modules:
  0.0 877.9 jit_solution(14026452026991364912)
XLA Ops:
  11.4 2.3 dynamic-slice_bitcast_fusion
  16.0 178.9 %shard_map.229 = (bf16[256,8,768]{2,1,0:T(8,128)(2,1)}, bf16[32,8,2048]{2,1,0:T(8,128)(2,1)}, bf16[256,8,2048]{2,1,0:T(8,128)(2,1)}, bf16[128,8,2048]{2,1,0:T(8,...) custom-call(bf16[4,16,8,2048]{3,2,1,0:T(8,128)(2,1)} %bitcast.131, ...), custom_call_target="tpu_custom_call" | custom-call | tf_op jit(solution)/shard_map/pallas_call | solution.py:404
  197.5 23.8 %shard_map.230 = (bf16[8,16,8,256]{3,2,1,0:T(8,128)(2,1)}, f32[1024,128]{1,0:T(8,128)}) custom-call(bf16[1024,768]{1,0:T(8,128)(2,1)} %bitcast.122, s32[8,1024]{1,0:T(8,128)} %add_add_fusion.info, s32[1024,128]{1,0:T(8,128)} %broadcast_in_dim.63.pcol), custom_call_target="tpu_custom_call" | custom-call | tf_op jit(solution)/shard_map/pallas_call | solution.py:502
  223.7 10.0 %fusion.10 = f32[1024,1024]{1,0:T(8,128)} fusion(bf16[1024,2048]{1,0:T(8,128)(2,1)} %bitcast.159, bf16[128,8,2048]{2,1,0:T(8,128)(2,1)} %get-tuple-element.44), kind=kOutput, calls=%fused_computation.69 | convolution fusion | flops 4294967296 | bytes 12582912 | tf_op jit(solution)/shard_map/nd,fd->nf/dot_general | solution.py:1189
  233.7 54.4 %shard_map.231 = (bf16[4,2,128,2048]{3,2,1,0:T(8,128)(2,1)}, f32[128,2048]{1,0:T(8,128)}, f32[8,128]{1,0:T(8,128)}) custom-call(bf16[4,256,256]{2,1,0:T(8,128)(2,1)} %bitcast.138, bf16[256,2048]{1,0:T(8,128)(2,1)} %bitcast.144, bf16[128,2048]{1,0:T(8,128)(2,1)} %get-tuple-element.89.x_own, f32[128,128]{1,0:T(8,128)} %broadcast_in_dim.65.keep, ...), custom_call_target="tpu_custom_call" | custom-call | tf_op jit(solution)/shard_map/pallas_call | solution.py:829
  289.3 8.1 fusion
  297.5 10.2 %multiply_convert_fusion.1 = (bf16[1024,1024]{1,0:T(8,128)(2,1)}, bf16[1024,1024]{1,0:T(8,128)(2,1)S(1)}, bf16[1024,1024]{1,0:T(8,128)(2,1)}) fusion(f32[1024,1024]{1,0:T(8,128)S(1)} %copy-done.12, f32[1024,1024]{1,0:T(8,128)S(1)} %fusion, bf16[1024,2048]{1,0:T(8,128)(2,1)S(1)} %bitcast.163, bf16[2048,2048]{1,0:T(8,128)(2,1)} %bitcast.118), kind=kOutput, calls=%fused_computation.14 | convolution fusion | flops 4311744512 | bytes 23068672 | tf_op jit(solution)/shard_map/dot_general | solution.py:1187
  307.7 6.2 convert_bitcast_fusion.1.refs_3_
  314.0 49.8 %shard_map.232 = (bf16[4,1,128,2048]{3,2,1,0:T(8,128)(2,1)}, f32[2,8,128]{2,1,0:T(8,128)}) custom-call(bf16[4,256,1024]{2,1,0:T(8,128)(2,1)} %bitcast.137, bf16[1024,2048]{1,0:T(8,128)(2,1)} %bitcast.129, f32[128,2048]{1,0:T(8,128)} %get-tuple-element.45.resid.resid_ref, f32[128,128]{1,0:T(8,128)} %broadcast_in_dim.65.keep), custom_call_target="tpu_custom_call" | custom-call | tf_op jit(solution)/shard_map/pallas_call | solution.py:856
  365.0 14.2 %convert_bitcast_fusion.refs_2_ = bf16[256,8,2048]{2,1,0:T(8,128)(2,1)} fusion(bf16[1024,2048]{1,0:T(8,128)(2,1)} %bitcast.162, bf16[1024,1024]{1,0:T(8,128)(2,1)} %get-tuple-element.68, bf16[1024,1024]{1,0:T(8,128)(2,1)S(1)} %copy-done.6), kind=kOutput, calls=%fused_computation.1 | convolution fusion | flops 8602517504 | bytes 16777216 | tf_op jit(solution)/shard_map/nd,nf->df/dot_general | solution.py:1209
  379.2 2.5 pad_maximum_fusion
  381.7 60.3 %shard_map.233 = (bf16[4,2,128,2048]{3,2,1,0:T(8,128)(2,1)}, f32[128,2048]{1,0:T(8,128)}, f32[8,2048]{1,0:T(8,128)}) custom-call(bf16[4,256,2048]{2,1,0:T(8,128)(2,1)} %bitcast.116, bf16[2048,2048]{1,0:T(8,128)(2,1)} %bitcast.119, f32[128,2048]{1,0:T(8,128)} %get-tuple-element.45.resid.resid_ref, bf16[128,2048]{1,0:T(8,128)(2,1)} %get-tuple-element.88.cot_own, ...), custom_call_target="tpu_custom_call" | custom-call | tf_op jit(solution)/shard_map/pallas_call | solution.py:884
  442.0 4.3 convolution_convert_fusion.1
  446.3 52.9 %shard_map.234 = bf16[8,16,8,768]{3,2,1,0:T(8,128)(2,1)} custom-call(bf16[8,16,8,256]{3,2,1,0:T(8,128)(2,1)} %bitcast.150, bf16[1024,768]{1,0:T(8,128)(2,1)} %bitcast.123, s32[8,1024]{1,0:T(8,128)} %add_add_fusion.info, s32[1024,128]{1,0:T(8,128)} %broadcast_in_dim.63.pcol, f32[1024,128]{1,0:T(8,128)} %get-tuple-element.49.lse, f32[1024,256]{1,0:T(8,128)} %copy.53.cos_ref, ...), custom_call_target="tpu_custom_call" | custom-call | tf_op jit(solution)/shard_map/pallas_call | solution.py:654
  499.2 2.3 reverse_select_fusion.3
  501.5 7.9 fusion.6.refs_0_
  509.5 53.7 %shard_map.235 = (bf16[4,1,128,2048]{3,2,1,0:T(8,128)(2,1)}, f32[8,2048]{1,0:T(8,128)}) custom-call(bf16[4,256,768]{2,1,0:T(8,128)(2,1)} %bitcast.121, bf16[2048,768]{1,0:T(8,128)(2,1)} %bitcast.133, bf16[128,2048]{1,0:T(8,128)(2,1)} %get-tuple-element.89.x_own, f32[128,2048]{1,0:T(8,128)} %get-tuple-element.51.grad_resid, f32[4,8,512]{2,1,0:T(8,128)} %get-tuple-element.41.gains), custom_call_target="tpu_custom_call" | custom-call | tf_op jit(solution)/shard_map/pallas_call | solution.py:912
  564.9 2.7 concatenate.47
  567.6 69.5 %psum.7 = f32[4224]{0:T(1024)S(1)} all-reduce(f32[4224]{0:T(1024)S(1)} %concatenate.47), channel_id=1, replica_groups=mesh['shard'=4,'context'=8,'tensor'=4] {'shard','context','tensor'}, use_global_device_ids=true, to_apply=%region_2.3 | all-reduce | flops 4224 | bytes 33792 | tf_op jit(solution)/shard_map/psum | solution.py:1242
  639.4 4.4 fusion.5.refs_1_
  643.8 209.5 %shard_map.236 = (bf16[2,2,64,8,512]{4,3,2,1,0:T(8,128)(2,1)}, bf16[2,2,32,8,2048]{4,3,2,1,0:T(8,128)(2,1)}, bf16[2,2,16,8,512]{4,3,2,1,0:T(8,128)(2,1)}, bf16[2,2,32,8,768]{4,3,2,1,0:T(8,128)(2,1)}) custom-call(bf16[256,8,768]{2,1,0:T(8,128)(2,1)} %fusion.6.refs_0_, bf16[32,8,2048]{2,1,0:T(8,128)(2,1)} %fusion.5.refs_1_, ...), custom_call_target="tpu_custom_call" | custom-call | tf_op jit(solution)/shard_map/pallas_call | solution.py:1093
  860.7 2.7 reverse_select_fusion.1
  869.1 2.3 pad_maximum_fusion.2
  871.4 2.3 pad_maximum_fusion.1
  (82 shorter events, 40.5 us)
Async XLA Ops:
  289.3 8.2 copy-start.11
  289.3 8.2 copy-start.12
  297.5 10.2 %copy-start.10 = (bf16[4,2,16,8,2048]{4,3,2,1,0:T(8,128)(2,1)S(1)}, bf16[4,2,16,8,2048]{4,3,2,1,0:T(8,128)(2,1)}, u32[]{:S(2)}) copy-start(bf16[4,2,16,8,2048]{4,3,2,1,0:T(8,128)(2,1)} %get-tuple-element.47) | copy-start | bytes 12582916
  307.7 6.2 copy-start.3
  314.0 51.1 %copy-start.6 = (bf16[1024,1024]{1,0:T(8,128)(2,1)S(1)}, bf16[1024,1024]{1,0:T(8,128)(2,1)}, u32[]{:S(2)}) copy-start(bf16[1024,1024]{1,0:T(8,128)(2,1)} %get-tuple-element.66) | copy-start | bytes 6291460
  365.0 14.2 %copy-start.7 = (bf16[1024,1024]{1,0:T(8,128)(2,1)S(1)}, bf16[1024,1024]{1,0:T(8,128)(2,1)}, u32[]{:S(2)}) copy-start(bf16[1024,1024]{1,0:T(8,128)(2,1)} %get-tuple-element.68) | copy-start | bytes 6291460
  381.7 60.3 %copy-start.9 = (bf16[32,8,2048]{2,1,0:T(8,128)(2,1)S(1)}, bf16[32,8,2048]{2,1,0:T(8,128)(2,1)}, u32[]{:S(2)}) copy-start(bf16[32,8,2048]{2,1,0:T(8,128)(2,1)} %get-tuple-element.40) | copy-start | bytes 3145732
  501.5 8.0 copy-start
  853.3 2.4 copy-start.8
  856.6 3.4 copy-start.2
  860.7 3.7 copy-start.1
  871.4 2.4 copy-start.4
  873.8 2.3 copy-start.5
